TPU v7x, 512 devices: a whole 4x8x8 slice. The times are simulated.
512 devices in a mesh: row: 8 (over z_lo, x), col: 8 (over z_hi, core), depth: 8 (over y).
Axes of the slice: x: 4, y: 8, z: 8 (z_hi: 4, z_lo: 2; z = z_hi * 2 + z_lo), core: 2. Of those that a mesh axis runs over, the one named last changes fastest.
Arguments:
- stream: bfloat16 [256, 8192], P(('row', 'depth'), 'col'), may hold values from -6 to 6
- norm_gain: float32 [8192], P('col'), may hold values from 0.5 to 1.5
- w_gate: bfloat16 [8192, 21504], P('col', ('row', 'depth')), may hold values from -0.0625 to 0.0625
- w_up: bfloat16 [8192, 21504], P('col', ('row', 'depth')), may hold values from -0.0625 to 0.0625
- w_down: bfloat16 [21504, 8192], P(('row', 'depth'), 'col'), may hold values from -0.0390625 to 0.0390625
- d_mixed: bfloat16 [256, 8192], P(('row', 'depth'), 'col'), may hold values from -6 to 6
Outputs:
- new_stream: bfloat16 [256, 8192], P(('row', 'depth'), 'col')
- grad_stream: bfloat16 [256, 8192], P(('row', 'depth'), 'col')
- grad_gate: bfloat16 [8192, 21504], P('col', ('row', 'depth'))
- grad_up: bfloat16 [8192, 21504], P('col', ('row', 'depth'))
- grad_down: bfloat16 [21504, 8192], P(('row', 'depth'), 'col')
All inputs are finite; a program needn't handle non-finite values.
Results may differ from a plain program's by a relative error of at most 0.0067.
Values may be sent and summed in bfloat16 or wider, within the bound.
A program may use at most 64 MiB of HBM per device.

v0:
```python
import jax
import jax.numpy as jnp
from jax import lax
from jax.sharding import PartitionSpec as P

D = 8192


epsilon = 1e-05


def contract_first(left, right):
    return lax.dot_general(
        left, right, (((0,), (0,)), ((), ())), preferred_element_type=jnp.float32
    )


def contract_last(left, right):
    return lax.dot_general(
        left, right, (((1,), (1,)), ((), ())), preferred_element_type=jnp.float32
    )


def on_device(stream, norm_gain, w_gate, w_up, w_down, d_mixed):
    hidden_local = w_gate.shape[1]
    stream_f = stream.astype(jnp.float32)
    square_sum = lax.psum(jnp.sum(stream_f * stream_f, axis=1), "col")
    inv_rms = lax.rsqrt(square_sum[:, None] / D + epsilon)
    normed = (stream_f * inv_rms * norm_gain[None, :]).astype(jnp.bfloat16)
    normed_all = lax.all_gather(normed, ("row", "depth"), axis=0, tiled=True)
    row_block = normed_all
    gate_share = lax.psum_scatter(
        jnp.concatenate(
            [
                jnp.dot(row_block, w_gate, preferred_element_type=jnp.float32),
                jnp.dot(row_block, w_up, preferred_element_type=jnp.float32),
            ],
            axis=1,
        ),
        "col",
        scatter_dimension=0,
        tiled=True,
    )
    gate = gate_share[:, :hidden_local]
    up_proj = gate_share[:, hidden_local:]
    sigmoid_gate = jax.nn.sigmoid(gate)
    activated = gate * sigmoid_gate
    hidden_share = (activated * up_proj).astype(jnp.bfloat16)
    hidden_all = lax.all_gather(hidden_share, "col", axis=0, tiled=True)
    row_block = hidden_all
    output_share = lax.psum_scatter(
        jnp.dot(row_block, w_down, preferred_element_type=jnp.float32),
        ("row", "depth"),
        scatter_dimension=0,
        tiled=True,
    )
    new_stream = (stream_f + output_share).astype(jnp.bfloat16)
    d_mixed_all = lax.all_gather(d_mixed, ("row", "depth"), axis=0, tiled=True)
    grad_down = contract_first(hidden_all, d_mixed_all).astype(jnp.bfloat16)
    row_block = d_mixed_all
    d_hidden = lax.psum_scatter(
        contract_last(row_block, w_down), "col", scatter_dimension=0, tiled=True
    )
    d_gate = (d_hidden * up_proj * sigmoid_gate * (1.0 + gate * (1.0 - sigmoid_gate))).astype(
        jnp.bfloat16
    )
    d_up = (d_hidden * activated).astype(jnp.bfloat16)
    d_gate_all, d_up_all = (
        lax.all_gather(d_gate, "col", axis=0, tiled=True),
        lax.all_gather(d_up, "col", axis=0, tiled=True),
    )
    grad_gate = contract_first(normed_all, d_gate_all).astype(jnp.bfloat16)
    grad_up = contract_first(normed_all, d_up_all).astype(jnp.bfloat16)
    d_normed = lax.psum_scatter(
        contract_last(d_gate_all, w_gate) + contract_last(d_up_all, w_up),
        ("row", "depth"),
        scatter_dimension=0,
        tiled=True,
    )
    d_scaled = d_normed * norm_gain[None, :]
    inner_sum = lax.psum(jnp.sum(d_scaled * stream_f, axis=1), "col")
    d_stream = inv_rms * d_scaled - stream_f * inv_rms**3 * inner_sum[:, None] / D
    grad_stream = (d_mixed.astype(jnp.float32) + d_stream).astype(jnp.bfloat16)
    return (new_stream, grad_stream, grad_gate, grad_up, grad_down)


def solution(mesh):
    placed = (
        P(("row", "depth"), "col"),
        P("col"),
        P("col", ("row", "depth")),
        P("col", ("row", "depth")),
        P(("row", "depth"), "col"),
        P(("row", "depth"), "col"),
    )
    return jax.shard_map(
        on_device,
        mesh=mesh,
        in_specs=placed,
        out_specs=(
            P(("row", "depth"), "col"),
            P(("row", "depth"), "col"),
            P("col", ("row", "depth")),
            P("col", ("row", "depth")),
            P(("row", "depth"), "col"),
        ),
        check_vma=False,
    )
```

profile of v0, /device:TPU:1, one launch (start us, length us, event | category | flops | bytes accessed | tf_op | source)
XLA Modules:
  0.0 1066.1 jit_solution(12665239490869809152)
XLA Ops:
  7.2 0.0 copy-start
  7.2 0.0 copy-start.2
  7.2 0.0 reduce-scatter.9.cloned.1.call-start
  7.2 0.9 fusion.1
  8.2 133.8 %all-gather.1 = bf16[64,4,1024]{2,1,0:T(4,128)(2,1)S(1)} all-gather(bf16[1,4,1024]{2,1,0:T(4,128)(2,1)} %bitcast.24), channel_id=1, replica_groups=mesh['row'=8,'col'=8,'depth'=8] {'row','depth'}, dimensions={0}, use_global_device_ids=true | all-gather | bytes 532480 | tf_op jit(solution)/shard_map/all_gather | solution.py:58
  142.0 0.1 reshape.22
  142.1 0.0 copy-done.2
  142.1 0.0 copy-start.4
  142.1 0.0 copy-start.5
  142.1 1.2 fusion.15
  143.3 0.0 reduce-scatter.9.cloned.1.call-update
  143.4 0.0 reduce-scatter.7.cloned.1.call-start
  143.4 46.1 %psum.14 = f32[4]{0:T(128)S(1)} all-reduce(f32[4]{0:T(128)S(1)} %fusion.1), channel_id=1, replica_groups=mesh['row'=8,'col'=8,'depth'=8] {'col'}, use_global_device_ids=true, to_apply=%region_1.0 | all-reduce | flops 4 | bytes 32 | tf_op jit(solution)/shard_map/psum | solution.py:27
  189.5 0.0 copy-done.4
  189.5 0.0 copy-done.5
  189.5 0.1 fusion.11
  189.6 124.8 %all-gather = bf16[64,4,1024]{2,1,0:T(4,128)(2,1)S(1)} all-gather(bf16[1,4,1024]{2,1,0:T(4,128)(2,1)S(1)} %fusion.11), channel_id=1, replica_groups=mesh['row'=8,'col'=8,'depth'=8] {'row','depth'}, dimensions={0}, use_global_device_ids=true | all-gather | bytes 532480 | tf_op jit(solution)/shard_map/all_gather | solution.py:30
  314.4 0.0 copy-start.1
  314.4 0.1 reshape.20
  314.5 0.0 copy-done
  314.5 0.4 fusion.12
  314.9 0.6 copy-done.1
  315.5 0.4 fusion.13
  315.9 1.2 copy.22
  317.1 0.0 reduce-scatter.7.cloned.1.call-update
  317.1 0.0 all-reduce.5.cloned.1.call-start
  317.1 0.0 reduce-scatter.9.cloned.1.call-done
  317.2 61.2 %reduce-scatter.7.cloned.1.call-done = f32[32,672]{1,0:T(8,128)} async-done(((f32[256,672]{1,0:T(8,128)}), f32[32,672]{1,0:T(8,128)}) %reduce-scatter.7.cloned.1.call-update) | async-done | bytes 86032 | tf_op jit(solution)/shard_map/reduce_scatter | solution.py:32
  378.4 1.0 multiply_convert_fusion
  379.4 16.5 %all_gather.18 = bf16[256,336]{1,0:T(8,128)(2,1)S(1)} all-gather(bf16[32,336]{1,0:T(8,128)(2,1)S(1)} %get-tuple-element.8), channel_id=1, replica_groups=mesh['row'=8,'col'=8,'depth'=8] {'col'}, dimensions={0}, use_global_device_ids=true | all-gather | bytes 193536 | tf_op jit(solution)/shard_map/all_gather | solution.py:69
  395.9 0.0 copy-start.3
  395.9 0.4 fusion.16
  396.3 14.7 %all_gather.19 = bf16[256,336]{1,0:T(8,128)(2,1)S(1)} all-gather(bf16[32,336]{1,0:T(8,128)(2,1)S(1)} %get-tuple-element.7), channel_id=1, replica_groups=mesh['row'=8,'col'=8,'depth'=8] {'col'}, dimensions={0}, use_global_device_ids=true | all-gather | bytes 193536 | tf_op jit(solution)/shard_map/all_gather | solution.py:70
  411.0 14.6 %all_gather.16 = bf16[256,336]{1,0:T(8,128)(2,1)S(1)} all-gather(bf16[32,336]{1,0:T(8,128)(2,1)S(1)} %get-tuple-element.9), channel_id=1, replica_groups=mesh['row'=8,'col'=8,'depth'=8] {'col'}, dimensions={0}, use_global_device_ids=true | all-gather | bytes 193536 | tf_op jit(solution)/shard_map/all_gather | solution.py:49
  425.6 0.0 copy-done.3
  425.6 1.4 fusion.14
  427.1 1.4 convolution_add_fusion
  428.5 0.0 all-reduce.5.cloned.1.call-update
  428.5 1.3 dynamic-slice
  430.4 1.2 convolution_convert_fusion.1
  431.7 1.2 convolution_convert_fusion.2
  432.9 0.0 copy-start.6
  432.9 562.7 %all-reduce.5.cloned.1.call-done = (f32[256,1024]{1,0:T(8,128)}, f32[256,1024]{1,0:T(8,128)}) async-done(((f32[256,1024]{1,0:T(8,128)}, f32[256,1024]{1,0:T(8,128)}), (f32[256,1024]{1,0:T(8,128)}, f32[256,1024]{1,0:T(8,128)})) %all-reduce.5.cloned.1.call-update) | async-done | bytes 2097168
  995.6 0.9 fusion.10
  996.5 1.2 convolution_convert_fusion
  997.7 60.4 %psum.15 = f32[4]{0:T(128)S(1)} all-reduce(f32[4]{0:T(128)S(1)} %fusion.10), channel_id=1, replica_groups=mesh['row'=8,'col'=8,'depth'=8] {'col'}, use_global_device_ids=true, to_apply=%region_7.0 | all-reduce | flops 4 | bytes 32 | tf_op jit(solution)/shard_map/psum | solution.py:81
  1058.1 0.0 copy-done.6
  1058.1 1.5 fusion.9
  (2 shorter events, 0.1 us)
Async XLA Ops:
  7.2 307.3 %copy-start = (bf16[1024,336]{0,1:T(8,128)(2,1)S(1)}, bf16[1024,336]{0,1:T(8,128)(2,1)}, u32[]{:S(2)}) copy-start(bf16[1024,336]{0,1:T(8,128)(2,1)} %param.8) | copy-start | bytes 2064388
  7.2 134.9 %copy-start.2 = (bf16[336,1024]{1,0:T(8,128)(2,1)S(1)}, bf16[336,1024]{1,0:T(8,128)(2,1)}, u32[]{:S(2)}) copy-start(bf16[336,1024]{1,0:T(8,128)(2,1)} %param.10) | copy-start | bytes 2064388
  7.2 310.0 %reduce-scatter.9.cloned.1.call-start = ((), (), s32[]{:S(2)}) async-start(), calls=%async_computation.3 | async-start | bytes 442368 | tf_op jit(solution)/shard_map/reduce_scatter | solution.py:61
  142.1 47.4 %copy-start.4 = (bf16[4,1024]{1,0:T(4,128)(2,1)S(1)}, bf16[4,1024]{1,0:T(4,128)(2,1)}, u32[]{:S(2)}) copy-start(bf16[4,1024]{1,0:T(4,128)(2,1)} %param.6) | copy-start | bytes 24580
  142.1 47.4 %copy-start.5 = (f32[1024]{0:T(1024)S(1)}, f32[1024]{0:T(1024)}, u32[]{:S(2)}) copy-start(f32[1024]{0:T(1024)} %param.7) | copy-start | bytes 12292
  143.4 235.0 %reduce-scatter.7.cloned.1.call-start = ((), (), s32[]{:S(2)}) async-start(), calls=%async_computation.2 | async-start | bytes 884736 | tf_op jit(solution)/shard_map/reduce_scatter | solution.py:32
  314.4 1.1 copy-start.1
  317.1 678.5 %all-reduce.5.cloned.1.call-start = ((), (), s32[]{:S(2)}) async-start(), calls=%async_computation.4 | async-start | bytes 4194304
  395.9 29.8 %copy-start.3 = (bf16[336,1024]{1,0:T(8,128)(2,1)S(1)}, bf16[336,1024]{1,0:T(8,128)(2,1)}, u32[]{:S(2)}) copy-start(bf16[336,1024]{1,0:T(8,128)(2,1)} %param.10) | copy-start | bytes 2064388
  432.9 625.3 %copy-start.6 = (bf16[4,1024]{1,0:T(4,128)(2,1)S(1)}, bf16[4,1024]{1,0:T(4,128)(2,1)}, u32[]{:S(2)}) copy-start(bf16[4,1024]{1,0:T(4,128)(2,1)} %param.11) | copy-start | bytes 24580
Sparse Core Ops, SparseCore 0:
  143.5 62.1 reduce-scatter.8
  317.2 61.1 reduce-scatter.6
  428.6 566.9 all-reduce.4
where the time goes:
time: 1070 us
  waiting for transfers between devices  624 us (58%)
  blocking collectives  411 us (38%)
  between operations  14.5 us (1%)
    unnamed x4, waiting for transfers between devices  563 us
    all_gather x1, blocking collectives, on_device(): d_mixed_all = lax.all_gather(d_mixed, ('row', 'depth'), axis=0, tiled=True)  134 us
    all_gather x1, blocking collectives, on_device(): normed_all = lax.all_gather(normed, ('row', 'depth'), axis=0, tiled=True)  125 us
    reduce_scatter x1, waiting for transfers between devices, on_device(): lax.psum_scatter(jnp.concatenate([jnp.dot(row_block, w_gate, preferred_el...  61.2 us
    psum x1, blocking collectives, on_device(): inner_sum = lax.psum(jnp.sum(d_scaled * stream_f, axis=1), 'col')  60.4 us
    psum x1, blocking collectives, on_device(): square_sum = lax.psum(jnp.sum(stream_f * stream_f, axis=1), 'col')  46.1 us
  transfers between devices with their start and end apart: 3, of which 2 were waited for; matrix products, arithmetic and copies ran while one was open for 1% of the time, Pallas kernels for 0%

commit v1 on v0

v1 whole, which is shorter than its diff:
```python
import functools

import jax
import jax.numpy as jnp
from jax import lax
from jax.experimental import pallas as pl
from jax.experimental.pallas import tpu as pltpu
from jax.sharding import PartitionSpec as P

F32, BF16 = jnp.float32, jnp.bfloat16
LANES = 128
EPSILON = 1e-05


def dot(a, b, dims=((1,), (0,))):
    return lax.dot_general(a, b, (dims, ((), ())), preferred_element_type=F32)


def kernel(
    sizes,
    stream_hbm, mixed_hbm, gain_hbm, wg_hbm, wu_hbm, wd_hbm,
    new_hbm, dstream_hbm, gg_hbm, gu_hbm, gd_hbm,
    stream_ref, mixed_ref, gain_ref, w_down, w_both,
    norm_parts, norm_all, mixed_parts, mixed_rows, mixed_all,
    partial, pair_out, pair_in, quad_out, quad_in,
    act_all, act_rows,
    out_send, out_recv, out_send2, out_recv2,
    dn_send, dn_recv, dn_send2, dn_recv2,
    new_out, dstream_out, gg_out, gu_out, gd_out,
    local_sem, send_sem, recv_sem,
):
    R, C, Y, fh, D = sizes
    mine, wide = stream_ref.shape
    fw = act_all.shape[2]
    low, high = fh // LANES * LANES, pl.cdiv(fh, LANES) * LANES
    spare = 3 * fh
    last = fw - LANES
    Z = C // 2
    tokens = R * Y * mine
    row, col, dep = (lax.axis_index(a) for a in ("row", "col", "depth"))
    zh, core = lax.div(col, 2), lax.rem(col, 2)
    sibling = zh * 2 + 1 - core

    barrier = pltpu.get_barrier_semaphore()
    for k in range(1, R):
        pl.semaphore_signal(barrier, 1, device_id={"row": lax.rem(row + k, R)})
    for k in range(1, Y):
        pl.semaphore_signal(barrier, 1, device_id={"depth": lax.rem(dep + k, Y)})
    for k in range(1, Z):
        pl.semaphore_signal(
            barrier, 1, device_id={"col": lax.rem(zh + k, Z) * 2 + core}
        )
    pl.semaphore_signal(barrier, 1, device_id={"col": sibling})

    loads = [
        pltpu.make_async_copy(a, b, local_sem.at[i])
        for i, (a, b) in enumerate([
            (stream_hbm, stream_ref),
            (gain_hbm, gain_ref),
            (mixed_hbm, mixed_ref),
            (wg_hbm, w_both.at[pl.ds(fh, fh)]),
            (wu_hbm, w_both.at[pl.ds(2 * fh, fh)]),
            (wd_hbm, w_down.at[pl.ds(0, fh)]),
        ])
    ]
    for copy in loads:
        copy.start()

    sent = []

    def send(src, dst, here, there, to):
        copy = pltpu.make_async_remote_copy(
            src_ref=src, dst_ref=dst,
            send_sem=send_sem.at[here], recv_sem=recv_sem.at[there], device_id=to,
        )
        copy.start()
        sent.append(copy)

    def receive(dst, slot, to):
        pltpu.make_async_remote_copy(
            src_ref=dst, dst_ref=dst,
            send_sem=send_sem.at[0], recv_sem=recv_sem.at[slot], device_id=to,
        ).wait_recv()

    def exchange(axis, base, source, target):
        me, n = (row, R) if axis == "row" else (dep, Y)
        others = [lax.rem(me + k, n) for k in range(1, n)]
        for k, p in enumerate(others):
            send(source(p), target(me), base + k, base + me, {axis: p})

        def finish():
            for p in others:
                receive(target(p), base + p, {axis: p})

        return finish

    base = iter(range(0, 96, 8))

    for copy in loads[:3]:
        copy.wait()
    stream = stream_ref[...].astype(F32)
    squares = jnp.sum(stream * stream, axis=1, keepdims=True)
    lane = lax.broadcasted_iota(jnp.int32, (mine, LANES), 1)
    norm_parts[row, :, 0:wide] = (stream * gain_ref[...]).astype(BF16)
    norm_parts[row, :, wide : wide + LANES] = jnp.where(
        lane == spare - last, squares, 0.0
    ).astype(BF16)
    mixed_parts[dep] = mixed_ref[...]

    pl.semaphore_wait(barrier, (R - 1) + (Y - 1) + (Z - 1) + 1)
    n1 = exchange("row", next(base), lambda p: norm_parts.at[row], lambda q: norm_parts.at[q])
    d1 = exchange("depth", next(base), lambda p: mixed_parts.at[dep], lambda q: mixed_parts.at[q])
    n1()
    norm_all[dep] = norm_parts[...].astype(F32).reshape(norm_all.shape[1:]).astype(BF16)
    n2 = exchange("depth", next(base), lambda p: norm_all.at[dep], lambda q: norm_all.at[q])
    d1()
    mixed_rows[row] = mixed_parts[...].astype(F32).reshape(mixed_rows.shape[1:]).astype(BF16)
    d2 = exchange("row", next(base), lambda p: mixed_rows.at[row], lambda q: mixed_rows.at[q])

    for copy in loads[3:]:
        copy.wait()
    w_down[fh:high, :] = jnp.zeros((high - fh, wide), BF16)
    w_both[low:fh, :] = jnp.zeros((fh - low, wide), BF16)
    w_both[spare:fw, :] = jnp.zeros((fw - spare, wide), BF16)
    t = lax.broadcasted_iota(jnp.int32, (tokens, tokens), 0)
    u = lax.broadcasted_iota(jnp.int32, (tokens, tokens), 1)
    by_row = ((t // mine) % R) * (Y * mine) + (t // (R * mine)) * mine + t % mine
    to_depth = (u == by_row).astype(F32).astype(BF16)
    by_depth = ((t // mine) % Y) * (R * mine) + (t // (Y * mine)) * mine + t % mine
    to_row = (u == by_depth).astype(F32).astype(BF16)

    n2()
    normed = norm_all[...].reshape(tokens, wide + LANES)
    both = dot(normed[:, 0:wide], w_both[low:fw, :], ((1,), (1,)))
    partial[:, :, low:fw] = both.reshape(Y, R * mine, fw - low)
    partial[:, :, last:fw] += norm_all[:, :, wide : wide + LANES].astype(F32)
    d2()
    mixed_all[...] = dot(to_depth, mixed_rows[...].reshape(tokens, wide)).astype(BF16)
    dh = dot(mixed_all[...], w_down[...], ((1,), (1,))).reshape(Y, R * mine, high)
    partial[:, :, 0:low] = dh[:, :, 0:low]
    partial[:, :, low:high] += dh[:, :, low:high]

    pair_base, quad_base, share_base, side_base = (next(base) for _ in range(4))
    others = [lax.rem(zh + k, Z) for k in range(1, Z)]
    for q in [*others, zh]:
        pair_out[q] = partial[q * 2 + 1 - core].astype(BF16)
        send(pair_out.at[q], pair_in.at[q], pair_base + q, pair_base + q, {"col": sibling})
    for q in others:
        receive(pair_in.at[q], pair_base + q, {"col": sibling})
        quad_out[q] = (partial[q * 2 + core] + pair_in[q].astype(F32)).astype(BF16)
        send(quad_out.at[q], quad_in.at[zh], quad_base + q, quad_base + zh, {"col": q * 2 + core})
    receive(pair_in.at[zh], pair_base + zh, {"col": sibling})
    total = partial[col] + pair_in[zh].astype(F32)
    for q in others:
        receive(quad_in.at[q], quad_base + q, {"col": q * 2 + core})
        total = total + quad_in[q].astype(F32)

    inv = lax.rsqrt(total[:, spare : spare + 1] / D + EPSILON)
    dh = total[:, 0:fh]
    gate = inv * total[:, fh : 2 * fh]
    up = inv * total[:, 2 * fh : 3 * fh]
    sigma = jax.nn.sigmoid(gate)
    act = gate * sigma
    d_gate = dh * up * sigma * (1.0 + gate * (1.0 - sigma))
    d_up = dh * act
    inner = inv * inv * jnp.sum(d_gate * gate + d_up * up, axis=1, keepdims=True)
    lane = lax.broadcasted_iota(jnp.int32, (total.shape[0], LANES), 1)
    act_all[col, :, last:fw] = jnp.where(lane == spare - last, inner, 0.0).astype(BF16)
    act_all[col, :, 0:fh] = (act * up).astype(BF16)
    act_all[col, :, fh : 2 * fh] = (inv * d_gate).astype(BF16)
    act_all[col, :, 2 * fh : 3 * fh] = (inv * d_up).astype(BF16)

    def pass_on(q):
        ours = act_all.at[q * 2 + core]
        send(ours, ours, side_base + q, side_base + q, {"col": sibling})

    for q in others:
        send(act_all.at[col], act_all.at[col], share_base + q, share_base + zh, {"col": q * 2 + core})
    pass_on(zh)
    for q in others:
        receive(act_all.at[q * 2 + core], share_base + q, {"col": q * 2 + core})
        pass_on(q)
    for q in [zh, *others]:
        receive(act_all.at[q * 2 + 1 - core], side_base + q, {"col": sibling})

    acts = act_all[...].reshape(tokens, fw)
    out_send[...] = dot(acts[:, 0:high], w_down[...]).astype(BF16).reshape(out_send.shape)
    o1 = exchange("depth", next(base), lambda p: out_send.at[p], lambda q: out_recv.at[q])
    act_rows[...] = dot(to_row, acts[:, low:fw]).astype(BF16)
    dn_send[:, :, 0:wide] = dot(act_rows[...], w_both[low:fw, :]).astype(BF16).reshape(R, Y * mine, wide)
    dn_send[:, :, wide : wide + LANES] = act_rows[:, last - low : fw - low].reshape(R, Y * mine, LANES)
    e1 = exchange("row", next(base), lambda p: dn_send.at[p], lambda q: dn_recv.at[q])
    out_recv[dep] = out_send[dep]
    dn_recv[row] = dn_send[row]

    flipped = jnp.transpose(acts)
    gd_out[...] = dot(flipped[0:fh], mixed_all[...]).astype(BF16)
    gg_out[...] = dot(flipped[fh : 2 * fh], normed[:, 0:wide]).astype(BF16)
    gu_out[...] = dot(flipped[2 * fh : 3 * fh], normed[:, 0:wide]).astype(BF16)
    stores = [
        pltpu.make_async_copy(gd_out, gd_hbm, local_sem.at[0]),
        pltpu.make_async_copy(gg_out, gg_hbm, local_sem.at[1]),
        pltpu.make_async_copy(gu_out, gu_hbm, local_sem.at[2]),
    ]
    for copy in stores:
        copy.start()

    def add(ref, n):
        total = ref[0].astype(F32)
        for q in range(1, n):
            total = total + ref[q].astype(F32)
        return total

    e1()
    total = add(dn_recv, R)
    for q in range(Y):
        dn_send2[q] = total[q * mine : (q + 1) * mine].astype(BF16)
    e2 = exchange("depth", next(base), lambda p: dn_send2.at[p], lambda q: dn_recv2.at[q])
    dn_recv2[dep] = dn_send2[dep]
    o1()
    total = add(out_recv, Y)
    for q in range(R):
        out_send2[q] = total[q * mine : (q + 1) * mine].astype(BF16)
    o2 = exchange("row", next(base), lambda p: out_send2.at[p], lambda q: out_recv2.at[q])
    out_recv2[row] = out_send2[row]

    e2()
    total = add(dn_recv2, Y)
    inner = total[:, wide + spare - last : wide + spare - last + 1]
    dstream_out[...] = (
        mixed_ref[...].astype(F32) + gain_ref[...] * total[:, 0:wide] - stream * (inner / D)
    ).astype(BF16)
    o2()
    new_out[...] = (stream + add(out_recv2, R)).astype(BF16)
    stores += [
        pltpu.make_async_copy(dstream_out, dstream_hbm, local_sem.at[3]),
        pltpu.make_async_copy(new_out, new_hbm, local_sem.at[4]),
    ]
    for copy in stores[3:]:
        copy.start()

    for copy in sent:
        copy.wait_send()
    for copy in stores:
        copy.wait()


def on_device(axes, stream, norm_gain, w_gate, w_up, w_down, d_mixed):
    R, C, Y = axes
    mine, wide = stream.shape
    fh = w_gate.shape[1]
    fw = (3 * fh // LANES + 1) * LANES
    low, high = fh // LANES * LANES, pl.cdiv(fh, LANES) * LANES
    width = wide + LANES
    tokens = R * Y * mine
    assert Y == C
    share = tokens // C
    Z = C // 2
    vmem = lambda *shape: pltpu.VMEM(shape, BF16)
    far = pl.BlockSpec(memory_space=pl.ANY)
    shape = lambda *a: jax.ShapeDtypeStruct(a, BF16)
    new, dstream, gg, gu, gd = pl.pallas_call(
        functools.partial(kernel, (R, C, Y, fh, wide * C)),
        out_shape=(
            shape(mine, wide),
            shape(mine, wide),
            shape(fh, wide),
            shape(fh, wide),
            shape(fh, wide),
        ),
        in_specs=[far] * 6,
        out_specs=[far] * 5,
        scratch_shapes=[
            vmem(mine, wide), vmem(mine, wide), pltpu.VMEM((1, wide), F32), vmem(high, wide), vmem(fw, wide),
            vmem(R, mine, width), vmem(Y, R * mine, width),
            vmem(Y, mine, wide), vmem(R, Y * mine, wide), vmem(tokens, wide),
            pltpu.VMEM((C, share, fw), F32),
            vmem(Z, share, fw), vmem(Z, share, fw), vmem(Z, share, fw), vmem(Z, share, fw),
            vmem(C, share, fw), vmem(tokens, fw - low),
            vmem(Y, R * mine, wide), vmem(Y, R * mine, wide), vmem(R, mine, wide), vmem(R, mine, wide),
            vmem(R, Y * mine, width), vmem(R, Y * mine, width), vmem(Y, mine, width), vmem(Y, mine, width),
            vmem(mine, wide), vmem(mine, wide), vmem(fh, wide), vmem(fh, wide), vmem(fh, wide),
            pltpu.SemaphoreType.DMA((6,)),
            pltpu.SemaphoreType.DMA((96,)),
            pltpu.SemaphoreType.DMA((96,)),
        ],
        compiler_params=pltpu.CompilerParams(
            collective_id=0, has_side_effects=True, vmem_limit_bytes=60 << 20
        ),
    )(stream, d_mixed, norm_gain.reshape(1, wide), w_gate.T, w_up.T, w_down)
    return new, dstream, gg.T, gu.T, gd


def solution(mesh):
    tokens, weights = P(("row", "depth"), "col"), P("col", ("row", "depth"))
    return jax.shard_map(
        functools.partial(on_device, tuple(mesh.shape[a] for a in ("row", "col", "depth"))),
        mesh=mesh,
        in_specs=(tokens, P("col"), weights, weights, tokens, tokens),
        out_specs=(tokens, tokens, weights, weights, tokens),
        check_vma=False,
    )
```

time: 1070 us -> 81.9 us (0.08)
  waiting for transfers between devices: 624 us -> 0 us
  blocking collectives: 411 us -> 0 us
  Pallas kernels: 0 us -> 74.7 us
  between operations: 14.5 us -> 0.65 us
    unnamed x4 -> x0, waiting for transfers between devices: 563 us -> none
    all_gather x5 -> x0, blocking collectives: 304 us -> none  [the longest x1 134 us: on_device(): d_mixed_all = lax.all_gather(d_mixed, ('row', 'depth'), axis=0, tiled=True)]
    psum x2 -> x0, blocking collectives: 106 us -> none  [the longest x1 60.4 us: on_device(): inner_sum = lax.psum(jnp.sum(d_scaled * stream_f, axis=1), 'col')]
    pallas_call x0 -> x1, Pallas kernels: none -> 74.7 us  [on_device(): pl.pallas_call(functools.partial(kernel, (R, C, Y, fh, wide * C)), out_sh...]
    reduce_scatter x2 -> x0, waiting for transfers between devices: 61.2 us -> none  [the longest x1 61.2 us: on_device(): lax.psum_scatter(jnp.concatenate([jnp.dot(row_block, w_gate, preferred_el...]
  transfers between devices with their start and end apart: 3 -> 0, of which waited for: 2 -> 0; matrix products, arithmetic and copies ran while one was open for 1% -> 0% of each run, Pallas kernels for 0% -> 0%
where the time goes in v1:
time: 81.9 us; the launch traced here: 81.6 us
  Pallas kernels  74.7 us (91%)
  local copies, waits for them, and re-layouts  6.24 us (8%)
    pallas_call x1, Pallas kernels, on_device(): pl.pallas_call(functools.partial(kernel, (R, C, Y, fh, wide * C)), out_sh...  74.7 us
    unnamed x13, local copies, waits for them, and re-layouts  6.24 us

profile of v1, /device:TPU:1, one launch (start us, length us, event | category | flops | bytes accessed | tf_op | source)
XLA Modules:
  0.0 81.6 jit_solution(12945775140327779743)
XLA Ops:
  0.6 74.7 %shard_map.101 = (bf16[4,1024]{1,0:T(4,128)(2,1)}, bf16[4,1024]{1,0:T(4,128)(2,1)}, bf16[336,1024]{1,0:T(8,128)(2,1)}, bf16[336,1024]{1,0:T(8,128)(2,1)}, bf16[336,1024]{1,0:T(8,128)(2,1)}) custom-call(bf16[4,1024]{1,0:T(4,128)(2,1)} %stream_hbm.1, bf16[4,1024]{1,0:T(4,128)(2,1)} %mixed_hbm.1, f32[1,1024]{1,0:T(1,128)} %bitcast.9, ...), custom_call_target="tpu_custom_call" | custom-call | tf_op jit(solution)/shard_map/pallas_call | solution.py:262
  75.3 0.0 copy-start.3
  75.3 0.7 copy-done.3
  76.0 0.0 copy-start.2
  76.0 0.6 copy.16
  76.6 0.1 copy-done.2
  76.7 0.6 copy.17
  77.3 0.0 copy-start.1
  77.3 2.1 %copy.18 = bf16[1024,336]{0,1:T(8,128)(2,1)} copy(bf16[1024,336]{0,1:T(8,128)(2,1)} %bitcast.8) | data formatting | bytes 1376256
  79.4 0.0 copy-done.1
  79.4 0.0 copy-start
  79.4 0.8 %copy.19 = bf16[1024,336]{0,1:T(8,128)(2,1)} copy(bf16[1024,336]{0,1:T(8,128)(2,1)S(1)} %bitcast.7) | data formatting | bytes 1376256
  80.2 0.5 copy-done
  80.7 0.8 %copy.20 = bf16[336,1024]{1,0:T(8,128)(2,1)} copy(bf16[336,1024]{1,0:T(8,128)(2,1)S(1)} %copy-done) | data formatting | bytes 1376256
Async XLA Ops:
  75.3 0.7 copy-start.3
  76.0 0.7 copy-start.2
  77.3 2.1 %copy-start.1 = (bf16[336,1024]{1,0:T(8,128)(2,1)S(1)}, bf16[336,1024]{1,0:T(8,128)(2,1)}, u32[]{:S(2)}) copy-start(bf16[336,1024]{1,0:T(8,128)(2,1)} %get-tuple-element.13) | copy-start | bytes 2064388
  79.4 1.3 %copy-start = (bf16[336,1024]{1,0:T(8,128)(2,1)S(1)}, bf16[336,1024]{1,0:T(8,128)(2,1)}, u32[]{:S(2)}) copy-start(bf16[336,1024]{1,0:T(8,128)(2,1)} %get-tuple-element.24) | copy-start | bytes 2064388

commit v2 on v1

v2 whole, which is shorter than its diff:
```python
import functools

import jax
import jax.numpy as jnp
from jax import lax
from jax.experimental import pallas as pl
from jax.experimental.pallas import tpu as pltpu
from jax.sharding import PartitionSpec as P

F32, BF16 = jnp.float32, jnp.bfloat16
LANES = 128
EPSILON = 1e-05


def dot(a, b, dims=((1,), (0,))):
    return lax.dot_general(a, b, (dims, ((), ())), preferred_element_type=F32)


def kernel(
    sizes,
    stream_hbm, mixed_hbm, gain_hbm, wg_hbm, wu_hbm, wd_hbm,
    new_hbm, dstream_hbm, gg_hbm, gu_hbm, gd_hbm,
    stream_ref, mixed_ref, gain_ref, w_down, w_both, wt_down, wt_both,
    norm_parts, norm_all, extra_parts, extra_rows, extra_all,
    partial, pair_in, quad_out, quad_in,
    act_all,
    out_send, out_recv, out_send2, out_recv2,
    dn_send, dn_recv, dn_send2, dn_recv2,
    new_out, dstream_out, gg_out, gu_out, gd_out,
    local_sem, send_sem, recv_sem,
):
    R, C, Y, fh, D = sizes
    mine, wide = stream_ref.shape
    head = norm_all.shape[3]
    fw = act_all.shape[4]
    low, high = fh // LANES * LANES, pl.cdiv(fh, LANES) * LANES
    spare = 3 * fh
    last = fw - LANES
    end = 2 * wide - head
    Z, X = C // 2, R // 2
    half = X * Y * mine
    row, col, dep = (lax.axis_index(a) for a in ("row", "col", "depth"))
    zh, core = lax.div(col, 2), lax.rem(col, 2)
    plane, x = lax.div(row, X), lax.rem(row, X)
    planes = (plane, 1 - plane)
    x_peers = [lax.rem(x + k, X) for k in range(1, X)]
    depths = [lax.rem(dep + k, Y) for k in range(1, Y)]
    others = [lax.rem(zh + k, Z) for k in range(1, Z)]
    across = (1 - plane) * X
    to_x = lambda q: {"row": plane * X + q}
    to_depth = lambda q: {"depth": q}
    to_plane = {"row": across + x}
    to_chip = lambda q: {"col": q * 2 + core}
    to_core = {"col": zh * 2 + 1 - core}
    peers = [to_plane, to_core]
    peers += [to_x(q) for q in x_peers] + [{"row": across + q} for q in x_peers]
    peers += [to_chip(q) for q in others] + [to_depth(q) for q in depths]
    peers += [{"row": across + x, "depth": q} for q in depths]
    barrier = pltpu.get_barrier_semaphore()
    for peer in peers:
        pl.semaphore_signal(barrier, 1, device_id=peer)

    loads = [
        pltpu.make_async_copy(a, b, local_sem.at[i])
        for i, (a, b) in enumerate([
            (stream_hbm, stream_ref),
            (gain_hbm, gain_ref),
            (mixed_hbm, mixed_ref),
            (wg_hbm, w_both.at[pl.ds(fh, fh)]),
            (wu_hbm, w_both.at[pl.ds(2 * fh, fh)]),
            (wd_hbm, w_down.at[pl.ds(0, fh)]),
        ])
    ]
    for copy in loads:
        copy.start()

    sent, slots, waited = [], iter(range(160)), []

    def take(n):
        return [next(slots) for _ in range(n)][0]

    def send(src, dst, slot, to):
        copy = pltpu.make_async_remote_copy(
            src_ref=src, dst_ref=dst,
            send_sem=send_sem.at[len(waited) + len(sent)], recv_sem=recv_sem.at[slot], device_id=to,
        )
        copy.start()
        sent.append(copy)

    def receive(dst, slot, to):
        pltpu.make_async_remote_copy(
            src_ref=dst, dst_ref=dst,
            send_sem=send_sem.at[0], recv_sem=recv_sem.at[slot], device_id=to,
        ).wait_recv()

    def drain():
        for copy in sent:
            copy.wait_send()
        waited.extend(sent)
        sent.clear()

    def exchange(others, me, to, source, target, n):
        slot = take(n)
        for q in others:
            send(source(q), target(me), slot + me, to(q))

        def finish():
            for q in others:
                receive(target(q), slot + q, to(q))

        return finish

    for copy in loads[:3]:
        copy.wait()
    stream = stream_ref[...].astype(F32)
    scaled = (stream * gain_ref[...]).astype(BF16)
    squares = jnp.sum(stream * stream, axis=1, keepdims=True)
    lane = lax.broadcasted_iota(jnp.int32, (mine, LANES), 1)
    norm_parts[x] = scaled[:, 0:head]
    extra_parts[dep, :, 0:wide] = mixed_ref[...]
    extra_parts[dep, :, wide:end] = scaled[:, head:wide]
    extra_parts[dep, :, end : end + LANES] = jnp.where(
        lane == spare - last, squares, 0.0
    ).astype(BF16)

    pl.semaphore_wait(barrier, len(peers))
    n1 = exchange(x_peers, x, to_x, lambda q: norm_parts.at[x], lambda q: norm_parts.at[q], X)
    d1 = exchange(depths, dep, to_depth, lambda q: extra_parts.at[dep], lambda q: extra_parts.at[q], Y)
    n1()
    norm_all[plane, dep] = norm_parts[...].astype(F32).reshape(norm_all.shape[2:]).astype(BF16)
    over = take(2)
    ours = norm_all.at[plane, dep]
    send(ours, ours, over, to_plane)

    def spread_norm(p):
        return exchange(depths, dep, to_depth, lambda q: norm_all.at[p, dep], lambda q: norm_all.at[p, q], Y)

    def spread_extra(p):
        return exchange(x_peers, x, to_x, lambda q: extra_rows.at[p, x], lambda q: extra_rows.at[p, q], X)

    n2 = [spread_norm(plane)]
    d1()
    extra_rows[plane, x] = extra_parts[...].astype(F32).reshape(extra_rows.shape[2:]).astype(BF16)
    ours = extra_rows.at[plane, x]
    send(ours, ours, over + 1, to_plane)
    d2 = [spread_extra(plane)]

    for copy in loads[3:]:
        copy.wait()
    w_down[fh:high, :] = jnp.zeros((high - fh, wide), BF16)
    w_both[low:fh, :] = jnp.zeros((fh - low, wide), BF16)
    w_both[spare:fw, :] = jnp.zeros((fw - spare, wide), BF16)
    wt_both[...] = jnp.transpose(w_both[low:fw, :])
    wt_down[...] = jnp.transpose(w_down[...])
    t = lax.broadcasted_iota(jnp.int32, (half, half), 0)
    u = lax.broadcasted_iota(jnp.int32, (half, half), 1)
    there = ((t // mine) % X) * (Y * mine) + (t // (X * mine)) * mine + t % mine
    by_depth = (u == there).astype(F32).astype(BF16)
    there = ((t // mine) % Y) * (X * mine) + (t // (Y * mine)) * mine + t % mine
    by_x = (u == there).astype(F32).astype(BF16)

    drain()
    receive(norm_all.at[1 - plane, dep], over, to_plane)
    n2.append(spread_norm(1 - plane))
    receive(extra_rows.at[1 - plane, x], over + 1, to_plane)
    d2.append(spread_extra(1 - plane))

    quad = []
    for h, p in enumerate(planes):
        n2[h]()
        d2[h]()
        extra = dot(by_depth, extra_rows[p].reshape(half, end + LANES)).astype(BF16)
        extra_all[p] = extra
        both = dot(norm_all[p].reshape(half, head), wt_both[0:head, :])
        both += dot(extra[:, wide:end], wt_both[head:wide, :])
        both = both.reshape(2, Z, X * mine, fw - low)
        partial[p, :, :, :, low:fw] = both
        partial[p, :, :, :, last:fw] += extra[:, end : end + LANES].astype(F32).reshape(2, Z, X * mine, LANES)
        dh = dot(extra[:, 0:wide], wt_down[...]).reshape(2, Z, X * mine, high)
        partial[p, :, :, :, 0:low] = dh[:, :, :, 0:low]
        partial[p, :, :, :, low:high] += dh[:, :, :, low:high]
        pair = take(1)
        send(partial.at[p, 1 - core], pair_in.at[p], pair, to_core)
        receive(pair_in.at[p], pair, to_core)
        for q in others:
            quad_out[p, q] = (partial[p, core, q] + pair_in[p, q]).astype(BF16)
        quad.append(exchange(others, zh, to_chip, lambda q: quad_out.at[p, q], lambda q, p=p: quad_in.at[p, q], Z))

    share = []
    for h, p in enumerate(planes):
        quad[h]()
        total = partial[p, core, zh] + pair_in[p, zh]
        for q in others:
            total = total + quad_in[p, q].astype(F32)
        inv = lax.rsqrt(total[:, spare : spare + 1] / D + EPSILON)
        dh = total[:, 0:fh]
        gate = inv * total[:, fh : 2 * fh]
        up = inv * total[:, 2 * fh : 3 * fh]
        sigma = jax.nn.sigmoid(gate)
        act = gate * sigma
        d_gate = dh * up * sigma * (1.0 + gate * (1.0 - sigma))
        d_up = dh * act
        inner = inv * inv * jnp.sum(d_gate * gate + d_up * up, axis=1, keepdims=True)
        lane = lax.broadcasted_iota(jnp.int32, (total.shape[0], LANES), 1)
        act_all[p, core, zh, :, last:fw] = jnp.where(lane == spare - last, inner, 0.0).astype(BF16)
        act_all[p, core, zh, :, 0:fh] = (act * up).astype(BF16)
        act_all[p, core, zh, :, fh : 2 * fh] = (inv * d_gate).astype(BF16)
        act_all[p, core, zh, :, 2 * fh : 3 * fh] = (inv * d_up).astype(BF16)
        share.append(exchange(others, zh, to_chip, lambda q: act_all.at[p, core, zh], lambda q, p=p: act_all.at[p, core, q], Z))

    e1, o1 = [], []
    for h, p in enumerate(planes):
        side = take(1)
        share[h]()
        send(act_all.at[p, core], act_all.at[p, core], side, to_core)
        receive(act_all.at[p, 1 - core], side, to_core)
        acts = act_all[p].reshape(half, fw)
        out_send[p] = dot(acts[:, 0:high], w_down[:, 0:head]).astype(BF16).reshape(Y, X * mine, head)
        o1.append(exchange(depths, dep, to_depth, lambda q: out_send.at[p, q], lambda q, p=p: out_recv.at[p, q], Y))
        acts = dot(by_x, acts).astype(BF16)
        dn_send[p, :, :, 0:wide] = dot(acts[:, low:fw], w_both[low:fw, :]).astype(BF16).reshape(X, Y * mine, wide)
        dn_send[p, :, :, wide:end] = dot(acts[:, 0:high], w_down[:, head:wide]).astype(BF16).reshape(X, Y * mine, wide - head)
        dn_send[p, :, :, end : end + LANES] = acts[:, last:fw].reshape(X, Y * mine, LANES)
        e1.append(exchange(x_peers, x, to_x, lambda q: dn_send.at[p, q], lambda q, p=p: dn_recv.at[p, q], X))
        out_recv[p, dep] = out_send[p, dep]
        dn_recv[p, x] = dn_send[p, x]

    flipped = jnp.transpose(act_all[...].reshape(2 * half, fw))
    extra = extra_all[...].reshape(2 * half, end + LANES)
    normed = norm_all[...].reshape(2 * half, head)
    gd_out[...] = dot(flipped[0:fh], extra[:, 0:wide]).astype(BF16)
    stores = [pltpu.make_async_copy(gd_out, gd_hbm, local_sem.at[0])]
    stores[0].start()
    for i, (out, hbm) in enumerate(((gg_out, gg_hbm), (gu_out, gu_hbm)), 1):
        out[:, 0:head] = dot(flipped[i * fh : (i + 1) * fh], normed).astype(BF16)
        out[:, head:wide] = dot(flipped[i * fh : (i + 1) * fh], extra[:, wide:end]).astype(BF16)
        stores.append(pltpu.make_async_copy(out, hbm, local_sem.at[i]))
        stores[i].start()

    def add(ref, n):
        total = ref[0].astype(F32)
        for q in range(1, n):
            total = total + ref[q].astype(F32)
        return total

    def split(total, ref, n):
        for q in range(n):
            ref[q] = total[q * mine : (q + 1) * mine].astype(BF16)

    e2, o2 = take(2 * Y), take(2 * X)
    for h, p in enumerate(planes):
        e1[h]()
        split(add(dn_recv.at[p], X), dn_send2.at[p], Y)
        for q in depths if h == 0 else [dep, *depths]:
            to = {"depth": q} if h == 0 else {"row": across + x, "depth": q}
            send(dn_send2.at[p, q], dn_recv2.at[plane, dep], e2 + plane * Y + dep, to)
        o1[h]()
        split(add(out_recv.at[p], Y), out_send2.at[p], X)
        for q in x_peers if h == 0 else [x, *x_peers]:
            send(out_send2.at[p, q], out_recv2.at[plane, x], o2 + plane * X + x, {"row": p * X + q})
    out_recv2[plane, x] = out_send2[plane, x]
    dn_recv2[plane, dep] = dn_send2[plane, dep]

    for h, p in enumerate(planes):
        for q in x_peers if h == 0 else [x, *x_peers]:
            receive(out_recv2.at[p, q], o2 + p * X + q, {"row": p * X + q})
    total = add(out_recv2.at[0], X) + add(out_recv2.at[1], X)
    new_out[:, 0:head] = (stream[:, 0:head] + total).astype(BF16)
    for h, p in enumerate(planes):
        for q in depths if h == 0 else [dep, *depths]:
            to = {"depth": q} if h == 0 else {"row": across + x, "depth": q}
            receive(dn_recv2.at[p, q], e2 + p * Y + q, to)
    total = add(dn_recv2.at[0], Y) + add(dn_recv2.at[1], Y)
    inner = total[:, end + spare - last : end + spare - last + 1]
    dstream_out[...] = (
        mixed_ref[...].astype(F32) + gain_ref[...] * total[:, 0:wide] - stream * (inner / D)
    ).astype(BF16)
    new_out[:, head:wide] = (stream[:, head:wide] + total[:, wide:end]).astype(BF16)
    stores += [
        pltpu.make_async_copy(dstream_out, dstream_hbm, local_sem.at[3]),
        pltpu.make_async_copy(new_out, new_hbm, local_sem.at[4]),
    ]
    for copy in stores[3:]:
        copy.start()

    drain()
    for copy in stores:
        copy.wait()


def hand_over(*refs):
    n = len(refs) // 3
    given, out, held, (sem,) = refs[:n], refs[n : 2 * n], refs[2 * n : 3 * n], refs[3 * n :]
    loads = [pltpu.make_async_copy(given[i], held[i], sem.at[i]) for i in range(n)]
    stores = [pltpu.make_async_copy(held[i], out[i], sem.at[n + i]) for i in range(n)]
    for copy in loads:
        copy.start()
    for load, store in zip(loads, stores):
        load.wait()
        store.start()
    for copy in stores:
        copy.wait()


def on_device(axes, stream, norm_gain, w_gate, w_up, w_down, d_mixed):
    R, C, Y = axes
    mine, wide = stream.shape
    fh = w_gate.shape[1]
    fw = (3 * fh // LANES + 1) * LANES
    low, high = fh // LANES * LANES, pl.cdiv(fh, LANES) * LANES
    head = wide // LANES * 3 // 4 * LANES
    both = 2 * wide - head + LANES
    Z, X = C // 2, R // 2
    assert Y == C
    half = X * Y * mine
    vmem = lambda *shape: pltpu.VMEM(shape, BF16)
    f32 = lambda *shape: pltpu.VMEM(shape, F32)
    far = pl.BlockSpec(memory_space=pltpu.HBM)
    shape = lambda *a: jax.ShapeDtypeStruct(a, BF16)
    shapes = (shape(mine, wide),) * 2 + (shape(fh, wide),) * 3
    outs = pl.pallas_call(
        functools.partial(kernel, (R, C, Y, fh, wide * C)),
        out_shape=shapes,
        in_specs=[far] * 6,
        out_specs=[far] * 5,
        scratch_shapes=[
            vmem(mine, wide), vmem(mine, wide), f32(1, wide),
            vmem(high, wide), vmem(fw, wide), vmem(wide, high), vmem(wide, fw - low),
            vmem(X, mine, head), vmem(2, Y, X * mine, head),
            vmem(Y, mine, both), vmem(2, X, Y * mine, both), vmem(2, half, both),
            f32(2, 2, Z, X * mine, fw), f32(2, Z, X * mine, fw),
            vmem(2, Z, X * mine, fw), vmem(2, Z, X * mine, fw),
            vmem(2, 2, Z, X * mine, fw),
            vmem(2, Y, X * mine, head), vmem(2, Y, X * mine, head), vmem(2, X, mine, head), vmem(2, X, mine, head),
            vmem(2, X, Y * mine, both), vmem(2, X, Y * mine, both), vmem(2, Y, mine, both), vmem(2, Y, mine, both),
            vmem(mine, wide), vmem(mine, wide), vmem(fh, wide), vmem(fh, wide), vmem(fh, wide),
            pltpu.SemaphoreType.DMA((6,)),
            pltpu.SemaphoreType.DMA((160,)),
            pltpu.SemaphoreType.DMA((160,)),
        ],
        compiler_params=pltpu.CompilerParams(
            collective_id=0, has_side_effects=True, vmem_limit_bytes=60 << 20
        ),
    )(stream, d_mixed, norm_gain.reshape(1, wide), w_gate.T, w_up.T, w_down)
    new, dstream, gg, gu, gd = pl.pallas_call(
        hand_over,
        out_shape=shapes,
        in_specs=[far] * 5,
        out_specs=[far] * 5,
        scratch_shapes=[*(vmem(*a.shape) for a in shapes), pltpu.SemaphoreType.DMA((10,))],
        compiler_params=pltpu.CompilerParams(vmem_limit_bytes=60 << 20),
    )(*outs)
    return new, dstream, gg.T, gu.T, gd


def solution(mesh):
    tokens, weights = P(("row", "depth"), "col"), P("col", ("row", "depth"))
    return jax.shard_map(
        functools.partial(on_device, tuple(mesh.shape[a] for a in ("row", "col", "depth"))),
        mesh=mesh,
        in_specs=(tokens, P("col"), weights, weights, tokens, tokens),
        out_specs=(tokens, tokens, weights, weights, tokens),
        check_vma=False,
    )
```

time: 81.9 us -> 65 us (0.79)
  Pallas kernels: 74.7 us -> 63.7 us
  local copies, waits for them, and re-layouts: 6.24 us -> 0 us
    pallas_call x1, Pallas kernels: 74.7 us -> 61.2 us  [on_device(): pl.pallas_call(functools.partial(kernel, (R, C, Y, fh, wide * C)), out_sh...]
    unnamed x13 -> x0, local copies, waits for them, and re-layouts: 6.24 us -> none
    pallas_call x0 -> x1, Pallas kernels: none -> 2.52 us  [on_device(): pl.pallas_call(hand_over, out_shape=shapes, in_specs=[far] * 5, out_specs...]
where the time goes in v2:
time: 65 us; the launch traced here: 64.3 us
  Pallas kernels  63.7 us (98%)
    pallas_call x1, Pallas kernels, on_device(): pl.pallas_call(functools.partial(kernel, (R, C, Y, fh, wide * C)), out_sh...  61.2 us
    pallas_call x1, Pallas kernels, on_device(): pl.pallas_call(hand_over, out_shape=shapes, in_specs=[far] * 5, out_specs...  2.52 us

profile of v2, /device:TPU:1, one launch (start us, length us, event | category | flops | bytes accessed | tf_op | source)
XLA Modules:
  0.0 64.3 jit_solution(13820693820981777318)
XLA Ops:
  0.6 61.2 %shard_map.101 = (bf16[4,1024]{1,0:T(4,128)(2,1)}, bf16[4,1024]{1,0:T(4,128)(2,1)}, bf16[336,1024]{1,0:T(8,128)(2,1)}, bf16[336,1024]{1,0:T(8,128)(2,1)}, bf16[336,1024]{1,0:T(8,128)(2,1)}) custom-call(bf16[4,1024]{1,0:T(4,128)(2,1)} %stream_hbm.1, bf16[4,1024]{1,0:T(4,128)(2,1)} %mixed_hbm.1, f32[1,1024]{1,0:T(1,128)} %bitcast.7, ...), custom_call_target="tpu_custom_call" | custom-call | tf_op jit(solution)/shard_map/pallas_call | solution.py:321
  61.8 2.5 %shard_map.102 = (bf16[4,1024]{1,0:T(4,128)(2,1)}, bf16[4,1024]{1,0:T(4,128)(2,1)}, bf16[336,1024]{1,0:T(8,128)(2,1)}, bf16[336,1024]{1,0:T(8,128)(2,1)}, bf16[336,1024]{1,0:T(8,128)(2,1)}) custom-call(bf16[4,1024]{1,0:T(4,128)(2,1)} %get-tuple-element.15.refs_0_, bf16[4,1024]{1,0:T(4,128)(2,1)} %get-tuple-element.16.refs_1_, ...), custom_call_target="tpu_custom_call" | custom-call | tf_op jit(solution)/shard_map/pallas_call | solution.py:345

commit v3 on v2

--- a/solution.py
+++ b/solution.py
@@ -19,14 +19,13 @@
 def kernel(
     sizes,
     stream_hbm, mixed_hbm, gain_hbm, wg_hbm, wu_hbm, wd_hbm,
-    new_hbm, dstream_hbm, gg_hbm, gu_hbm, gd_hbm,
+    new_out, dstream_out, gg_out, gu_out, gd_out,
     stream_ref, mixed_ref, gain_ref, w_down, w_both, wt_down, wt_both,
     norm_parts, norm_all, extra_parts, extra_rows, extra_all,
     partial, pair_in, quad_out, quad_in,
     act_all,
     out_send, out_recv, out_send2, out_recv2,
     dn_send, dn_recv, dn_send2, dn_recv2,
-    new_out, dstream_out, gg_out, gu_out, gd_out,
     local_sem, send_sem, recv_sem,
 ):
     R, C, Y, fh, D = sizes
@@ -43,9 +42,24 @@
     zh, core = lax.div(col, 2), lax.rem(col, 2)
     plane, x = lax.div(row, X), lax.rem(row, X)
     planes = (plane, 1 - plane)
-    x_peers = [lax.rem(x + k, X) for k in range(1, X)]
-    depths = [lax.rem(dep + k, Y) for k in range(1, Y)]
-    others = [lax.rem(zh + k, Z) for k in range(1, Z)]
+    loads = [
+        pltpu.make_async_copy(a, b, local_sem.at[i])
+        for i, (a, b) in enumerate([
+            (stream_hbm, stream_ref),
+            (gain_hbm, gain_ref),
+            (mixed_hbm, mixed_ref),
+            (wg_hbm, w_both.at[pl.ds(fh, fh)]),
+            (wu_hbm, w_both.at[pl.ds(2 * fh, fh)]),
+            (wd_hbm, w_down.at[pl.ds(0, fh)]),
+        ])
+    ]
+    for copy in loads[:3]:
+        copy.start()
+
+    far = lambda n: sorted(range(1, n), key=lambda k: abs(k - n // 2))
+    x_peers = [lax.rem(x + k, X) for k in far(X)]
+    depths = [lax.rem(dep + k, Y) for k in far(Y)]
+    others = [lax.rem(zh + k, Z) for k in far(Z)]
     across = (1 - plane) * X
     to_x = lambda q: {"row": plane * X + q}
     to_depth = lambda q: {"depth": q}
@@ -59,19 +73,7 @@
     barrier = pltpu.get_barrier_semaphore()
     for peer in peers:
         pl.semaphore_signal(barrier, 1, device_id=peer)
-
-    loads = [
-        pltpu.make_async_copy(a, b, local_sem.at[i])
-        for i, (a, b) in enumerate([
-            (stream_hbm, stream_ref),
-            (gain_hbm, gain_ref),
-            (mixed_hbm, mixed_ref),
-            (wg_hbm, w_both.at[pl.ds(fh, fh)]),
-            (wu_hbm, w_both.at[pl.ds(2 * fh, fh)]),
-            (wd_hbm, w_down.at[pl.ds(0, fh)]),
-        ])
-    ]
-    for copy in loads:
+    for copy in loads[3:]:
         copy.start()
 
     sent, slots, waited = [], iter(range(160)), []
@@ -93,11 +95,11 @@
             send_sem=send_sem.at[0], recv_sem=recv_sem.at[slot], device_id=to,
         ).wait_recv()
 
-    def drain():
-        for copy in sent:
+    def drain(n=None):
+        for copy in sent[:n]:
             copy.wait_send()
-        waited.extend(sent)
-        sent.clear()
+        waited.extend(sent[:n])
+        del sent[:n]
 
     def exchange(others, me, to, source, target, n):
         slot = take(n)
@@ -159,7 +161,7 @@
     there = ((t // mine) % Y) * (X * mine) + (t // (Y * mine)) * mine + t % mine
     by_x = (u == there).astype(F32).astype(BF16)
 
-    drain()
+    drain(-3)
     receive(norm_all.at[1 - plane, dep], over, to_plane)
     n2.append(spread_norm(1 - plane))
     receive(extra_rows.at[1 - plane, x], over + 1, to_plane)
@@ -225,17 +227,15 @@
         out_recv[p, dep] = out_send[p, dep]
         dn_recv[p, x] = dn_send[p, x]
 
+    drain(-(len(depths) + len(x_peers)))
+
     flipped = jnp.transpose(act_all[...].reshape(2 * half, fw))
     extra = extra_all[...].reshape(2 * half, end + LANES)
     normed = norm_all[...].reshape(2 * half, head)
     gd_out[...] = dot(flipped[0:fh], extra[:, 0:wide]).astype(BF16)
-    stores = [pltpu.make_async_copy(gd_out, gd_hbm, local_sem.at[0])]
-    stores[0].start()
-    for i, (out, hbm) in enumerate(((gg_out, gg_hbm), (gu_out, gu_hbm)), 1):
+    for i, out in ((1, gg_out), (2, gu_out)):
         out[:, 0:head] = dot(flipped[i * fh : (i + 1) * fh], normed).astype(BF16)
         out[:, head:wide] = dot(flipped[i * fh : (i + 1) * fh], extra[:, wide:end]).astype(BF16)
-        stores.append(pltpu.make_async_copy(out, hbm, local_sem.at[i]))
-        stores[i].start()
 
     def add(ref, n):
         total = ref[0].astype(F32)
@@ -276,29 +276,16 @@
         mixed_ref[...].astype(F32) + gain_ref[...] * total[:, 0:wide] - stream * (inner / D)
     ).astype(BF16)
     new_out[:, head:wide] = (stream[:, head:wide] + total[:, wide:end]).astype(BF16)
-    stores += [
-        pltpu.make_async_copy(dstream_out, dstream_hbm, local_sem.at[3]),
-        pltpu.make_async_copy(new_out, new_hbm, local_sem.at[4]),
-    ]
-    for copy in stores[3:]:
+
+    drain()
+
+
+def hand_over(*refs):
+    n = len(refs) // 2
+    copies = [pltpu.make_async_copy(refs[i], refs[n + i], refs[2 * n].at[i]) for i in range(n)]
+    for copy in copies:
         copy.start()
-
-    drain()
-    for copy in stores:
-        copy.wait()
-
-
-def hand_over(*refs):
-    n = len(refs) // 3
-    given, out, held, (sem,) = refs[:n], refs[n : 2 * n], refs[2 * n : 3 * n], refs[3 * n :]
-    loads = [pltpu.make_async_copy(given[i], held[i], sem.at[i]) for i in range(n)]
-    stores = [pltpu.make_async_copy(held[i], out[i], sem.at[n + i]) for i in range(n)]
-    for copy in loads:
-        copy.start()
-    for load, store in zip(loads, stores):
-        load.wait()
-        store.start()
-    for copy in stores:
+    for copy in copies:
         copy.wait()
 
 
@@ -315,14 +302,15 @@
     half = X * Y * mine
     vmem = lambda *shape: pltpu.VMEM(shape, BF16)
     f32 = lambda *shape: pltpu.VMEM(shape, F32)
+    near = pl.BlockSpec(memory_space=pltpu.VMEM)
     far = pl.BlockSpec(memory_space=pltpu.HBM)
     shape = lambda *a: jax.ShapeDtypeStruct(a, BF16)
     shapes = (shape(mine, wide),) * 2 + (shape(fh, wide),) * 3
     outs = pl.pallas_call(
         functools.partial(kernel, (R, C, Y, fh, wide * C)),
-        out_shape=shapes,
+        out_shape=tuple(pltpu.VMEM(a.shape, BF16) for a in shapes),
         in_specs=[far] * 6,
-        out_specs=[far] * 5,
+        out_specs=[near] * 5,
         scratch_shapes=[
             vmem(mine, wide), vmem(mine, wide), f32(1, wide),
             vmem(high, wide), vmem(fw, wide), vmem(wide, high), vmem(wide, fw - low),
@@ -333,22 +321,21 @@
             vmem(2, 2, Z, X * mine, fw),
             vmem(2, Y, X * mine, head), vmem(2, Y, X * mine, head), vmem(2, X, mine, head), vmem(2, X, mine, head),
             vmem(2, X, Y * mine, both), vmem(2, X, Y * mine, both), vmem(2, Y, mine, both), vmem(2, Y, mine, both),
-            vmem(mine, wide), vmem(mine, wide), vmem(fh, wide), vmem(fh, wide), vmem(fh, wide),
             pltpu.SemaphoreType.DMA((6,)),
             pltpu.SemaphoreType.DMA((160,)),
             pltpu.SemaphoreType.DMA((160,)),
         ],
         compiler_params=pltpu.CompilerParams(
-            collective_id=0, has_side_effects=True, vmem_limit_bytes=60 << 20
+            collective_id=0, has_side_effects=True, vmem_limit_bytes=61 << 20
         ),
     )(stream, d_mixed, norm_gain.reshape(1, wide), w_gate.T, w_up.T, w_down)
     new, dstream, gg, gu, gd = pl.pallas_call(
         hand_over,
         out_shape=shapes,
-        in_specs=[far] * 5,
+        in_specs=[near] * 5,
         out_specs=[far] * 5,
-        scratch_shapes=[*(vmem(*a.shape) for a in shapes), pltpu.SemaphoreType.DMA((10,))],
-        compiler_params=pltpu.CompilerParams(vmem_limit_bytes=60 << 20),
+        scratch_shapes=[pltpu.SemaphoreType.DMA((5,))],
+        compiler_params=pltpu.CompilerParams(vmem_limit_bytes=1 << 20),
     )(*outs)
     return new, dstream, gg.T, gu.T, gd
 

time: 65 us -> 61.7 us (0.949)
  Pallas kernels: 63.7 us -> 60.9 us
    pallas_call x1, Pallas kernels: 61.2 us -> 59.6 us  [on_device(): pl.pallas_call(functools.partial(kernel, (R, C, Y, fh, wide * C)), out_sh...]
    pallas_call x1, Pallas kernels: 2.52 us -> 1.36 us  [on_device(): pl.pallas_call(hand_over, out_shape=shapes, in_specs=[near] * 5, out_spec...]
where the time goes in v3:
time: 61.7 us; the launch traced here: 61.6 us
  Pallas kernels  60.9 us (99%)
  between operations  0.64 us (1%)
    pallas_call x1, Pallas kernels, on_device(): pl.pallas_call(functools.partial(kernel, (R, C, Y, fh, wide * C)), out_sh...  59.6 us
    pallas_call x1, Pallas kernels, on_device(): pl.pallas_call(hand_over, out_shape=shapes, in_specs=[near] * 5, out_spec...  1.36 us

profile of v3, /device:TPU:1, one launch (start us, length us, event | category | flops | bytes accessed | tf_op | source)
XLA Modules:
  0.0 61.6 jit_solution(15907617448056854556)
XLA Ops:
  0.6 59.6 %shard_map.101 = (bf16[4,1024]{1,0:T(4,128)(2,1)S(1)}, bf16[4,1024]{1,0:T(4,128)(2,1)S(1)}, bf16[336,1024]{1,0:T(8,128)(2,1)S(1)}, bf16[336,1024]{1,0:T(8,128)(2,1)S(1)}, bf16[336,1024]{1,0:T(8,128)(2,1)S(1)}) custom-call(bf16[4,1024]{1,0:T(4,128)(2,1)} %stream_hbm.1, bf16[4,1024]{1,0:T(4,128)(2,1)} %mixed_hbm.1, f32[1,1024]{1,0:T(1,128)} %bitcast.7, ...), custom_call_target="tpu_custom_call" | custom-call | tf_op jit(solution)/shard_map/pallas_call | solution.py:309
  60.2 1.4 %shard_map.102 = (bf16[4,1024]{1,0:T(4,128)(2,1)}, bf16[4,1024]{1,0:T(4,128)(2,1)}, bf16[336,1024]{1,0:T(8,128)(2,1)}, bf16[336,1024]{1,0:T(8,128)(2,1)}, bf16[336,1024]{1,0:T(8,128)(2,1)}) custom-call(bf16[4,1024]{1,0:T(4,128)(2,1)S(1)} %get-tuple-element.15.refs_0_, bf16[4,1024]{1,0:T(4,128)(2,1)S(1)} %get-tuple-element.16.refs_1_, ...), custom_call_target="tpu_custom_call" | custom-call | tf_op jit(solution)/shard_map/pallas_call | solution.py:332

commit v4 on v3

--- a/solution.py
+++ b/solution.py
@@ -71,7 +71,7 @@
     peers += [to_chip(q) for q in others] + [to_depth(q) for q in depths]
     peers += [{"row": across + x, "depth": q} for q in depths]
     barrier = pltpu.get_barrier_semaphore()
-    for peer in peers:
+    for peer in reversed(peers):
         pl.semaphore_signal(barrier, 1, device_id=peer)
     for copy in loads[3:]:
         copy.start()
@@ -121,9 +121,10 @@
     norm_parts[x] = scaled[:, 0:head]
     extra_parts[dep, :, 0:wide] = mixed_ref[...]
     extra_parts[dep, :, wide:end] = scaled[:, head:wide]
-    extra_parts[dep, :, end : end + LANES] = jnp.where(
-        lane == spare - last, squares, 0.0
-    ).astype(BF16)
+    rounded = squares.astype(BF16).astype(F32)
+    first = spare - last + 2 * core
+    rest = jnp.where(lane == first + 1, squares - rounded, 0.0)
+    extra_parts[dep, :, end : end + LANES] = jnp.where(lane == first, rounded, rest).astype(BF16)
 
     pl.semaphore_wait(barrier, len(peers))
     n1 = exchange(x_peers, x, to_x, lambda q: norm_parts.at[x], lambda q: norm_parts.at[q], X)
@@ -169,17 +170,17 @@
 
     quad = []
     for h, p in enumerate(planes):
-        n2[h]()
         d2[h]()
         extra = dot(by_depth, extra_rows[p].reshape(half, end + LANES)).astype(BF16)
         extra_all[p] = extra
-        both = dot(norm_all[p].reshape(half, head), wt_both[0:head, :])
-        both += dot(extra[:, wide:end], wt_both[head:wide, :])
+        both = dot(extra[:, wide:end], wt_both[head:wide, :])
+        dh = dot(extra[:, 0:wide], wt_down[...]).reshape(2, Z, X * mine, high)
+        partial[p, :, :, :, 0:low] = dh[:, :, :, 0:low]
+        n2[h]()
+        both += dot(norm_all[p].reshape(half, head), wt_both[0:head, :])
         both = both.reshape(2, Z, X * mine, fw - low)
         partial[p, :, :, :, low:fw] = both
         partial[p, :, :, :, last:fw] += extra[:, end : end + LANES].astype(F32).reshape(2, Z, X * mine, LANES)
-        dh = dot(extra[:, 0:wide], wt_down[...]).reshape(2, Z, X * mine, high)
-        partial[p, :, :, :, 0:low] = dh[:, :, :, 0:low]
         partial[p, :, :, :, low:high] += dh[:, :, :, low:high]
         pair = take(1)
         send(partial.at[p, 1 - core], pair_in.at[p], pair, to_core)
@@ -194,7 +195,8 @@
         total = partial[p, core, zh] + pair_in[p, zh]
         for q in others:
             total = total + quad_in[p, q].astype(F32)
-        inv = lax.rsqrt(total[:, spare : spare + 1] / D + EPSILON)
+        squares = sum(total[:, spare + i : spare + i + 1] for i in range(4))
+        inv = lax.rsqrt(squares / D + EPSILON)
         dh = total[:, 0:fh]
         gate = inv * total[:, fh : 2 * fh]
         up = inv * total[:, 2 * fh : 3 * fh]
@@ -251,23 +253,23 @@
     for h, p in enumerate(planes):
         e1[h]()
         split(add(dn_recv.at[p], X), dn_send2.at[p], Y)
-        for q in depths if h == 0 else [dep, *depths]:
+        for q in depths if h == 0 else [*depths, dep]:
             to = {"depth": q} if h == 0 else {"row": across + x, "depth": q}
             send(dn_send2.at[p, q], dn_recv2.at[plane, dep], e2 + plane * Y + dep, to)
         o1[h]()
         split(add(out_recv.at[p], Y), out_send2.at[p], X)
-        for q in x_peers if h == 0 else [x, *x_peers]:
+        for q in x_peers if h == 0 else [*x_peers, x]:
             send(out_send2.at[p, q], out_recv2.at[plane, x], o2 + plane * X + x, {"row": p * X + q})
     out_recv2[plane, x] = out_send2[plane, x]
     dn_recv2[plane, dep] = dn_send2[plane, dep]
 
     for h, p in enumerate(planes):
-        for q in x_peers if h == 0 else [x, *x_peers]:
+        for q in x_peers if h == 0 else [*x_peers, x]:
             receive(out_recv2.at[p, q], o2 + p * X + q, {"row": p * X + q})
     total = add(out_recv2.at[0], X) + add(out_recv2.at[1], X)
     new_out[:, 0:head] = (stream[:, 0:head] + total).astype(BF16)
     for h, p in enumerate(planes):
-        for q in depths if h == 0 else [dep, *depths]:
+        for q in depths if h == 0 else [*depths, dep]:
             to = {"depth": q} if h == 0 else {"row": across + x, "depth": q}
             receive(dn_recv2.at[p, q], e2 + p * Y + q, to)
     total = add(dn_recv2.at[0], Y) + add(dn_recv2.at[1], Y)

time: 61.7 us -> 61.6 us (level)
  no operation moved by 1% of the time
where the time goes in v4:
time: 61.6 us; the launch traced here: 61.5 us
  Pallas kernels  60.8 us (99%)
  between operations  0.64 us (1%)
    pallas_call x1, Pallas kernels, on_device(): pl.pallas_call(functools.partial(kernel, (R, C, Y, fh, wide * C)), out_sh...  59.5 us
    pallas_call x1, Pallas kernels, on_device(): pl.pallas_call(hand_over, out_shape=shapes, in_specs=[near] * 5, out_spec...  1.36 us

profile of v4, /device:TPU:1, one launch (start us, length us, event | category | flops | bytes accessed | tf_op | source)
XLA Modules:
  0.0 61.5 jit_solution(4933269709696467005)
XLA Ops:
  0.6 59.5 %shard_map.101 = (bf16[4,1024]{1,0:T(4,128)(2,1)S(1)}, bf16[4,1024]{1,0:T(4,128)(2,1)S(1)}, bf16[336,1024]{1,0:T(8,128)(2,1)S(1)}, bf16[336,1024]{1,0:T(8,128)(2,1)S(1)}, bf16[336,1024]{1,0:T(8,128)(2,1)S(1)}) custom-call(bf16[4,1024]{1,0:T(4,128)(2,1)} %stream_hbm.1, bf16[4,1024]{1,0:T(4,128)(2,1)} %mixed_hbm.1, f32[1,1024]{1,0:T(1,128)} %bitcast.7, ...), custom_call_target="tpu_custom_call" | custom-call | tf_op jit(solution)/shard_map/pallas_call | solution.py:311
  60.1 1.4 %shard_map.102 = (bf16[4,1024]{1,0:T(4,128)(2,1)}, bf16[4,1024]{1,0:T(4,128)(2,1)}, bf16[336,1024]{1,0:T(8,128)(2,1)}, bf16[336,1024]{1,0:T(8,128)(2,1)}, bf16[336,1024]{1,0:T(8,128)(2,1)}) custom-call(bf16[4,1024]{1,0:T(4,128)(2,1)S(1)} %get-tuple-element.15.refs_0_, bf16[4,1024]{1,0:T(4,128)(2,1)S(1)} %get-tuple-element.16.refs_1_, ...), custom_call_target="tpu_custom_call" | custom-call | tf_op jit(solution)/shard_map/pallas_call | solution.py:334

commit v5 on v4

--- a/solution.py
+++ b/solution.py
@@ -106,8 +106,8 @@
         for q in others:
             send(source(q), target(me), slot + me, to(q))
 
-        def finish():
-            for q in others:
+        def finish(only=others):
+            for q in only:
                 receive(target(q), slot + q, to(q))
 
         return finish
@@ -214,10 +214,14 @@
 
     e1, o1 = [], []
     for h, p in enumerate(planes):
-        side = take(1)
-        share[h]()
-        send(act_all.at[p, core], act_all.at[p, core], side, to_core)
-        receive(act_all.at[p, 1 - core], side, to_core)
+        side = take(Z)
+        for q in [zh, *others[1:], others[0]]:
+            if q is not zh:
+                share[h]([q])
+            ours = act_all.at[p, core, q]
+            send(ours, ours, side + q, to_core)
+        for q in [zh, *others]:
+            receive(act_all.at[p, 1 - core, q], side + q, to_core)
         acts = act_all[p].reshape(half, fw)
         out_send[p] = dot(acts[:, 0:high], w_down[:, 0:head]).astype(BF16).reshape(Y, X * mine, head)
         o1.append(exchange(depths, dep, to_depth, lambda q: out_send.at[p, q], lambda q, p=p: out_recv.at[p, q], Y))

time: 61.6 us -> 61.6 us (level)
  no operation moved by 1% of the time
where the time goes in v5:
time: 61.6 us; the launch traced here: 61.5 us
  Pallas kernels  60.8 us (99%)
  between operations  0.64 us (1%)
    pallas_call x1, Pallas kernels, on_device(): pl.pallas_call(functools.partial(kernel, (R, C, Y, fh, wide * C)), out_sh...  59.5 us
    pallas_call x1, Pallas kernels, on_device(): pl.pallas_call(hand_over, out_shape=shapes, in_specs=[near] * 5, out_spec...  1.36 us

profile of v5, /device:TPU:1, one launch (start us, length us, event | category | flops | bytes accessed | tf_op | source)
XLA Modules:
  0.0 61.5 jit_solution(4125090280226341759)
XLA Ops:
  0.6 59.5 %shard_map.101 = (bf16[4,1024]{1,0:T(4,128)(2,1)S(1)}, bf16[4,1024]{1,0:T(4,128)(2,1)S(1)}, bf16[336,1024]{1,0:T(8,128)(2,1)S(1)}, bf16[336,1024]{1,0:T(8,128)(2,1)S(1)}, bf16[336,1024]{1,0:T(8,128)(2,1)S(1)}) custom-call(bf16[4,1024]{1,0:T(4,128)(2,1)} %stream_hbm.1, bf16[4,1024]{1,0:T(4,128)(2,1)} %mixed_hbm.1, f32[1,1024]{1,0:T(1,128)} %bitcast.7, ...), custom_call_target="tpu_custom_call" | custom-call | tf_op jit(solution)/shard_map/pallas_call | solution.py:315
  60.1 1.4 %shard_map.102 = (bf16[4,1024]{1,0:T(4,128)(2,1)}, bf16[4,1024]{1,0:T(4,128)(2,1)}, bf16[336,1024]{1,0:T(8,128)(2,1)}, bf16[336,1024]{1,0:T(8,128)(2,1)}, bf16[336,1024]{1,0:T(8,128)(2,1)}) custom-call(bf16[4,1024]{1,0:T(4,128)(2,1)S(1)} %get-tuple-element.15.refs_0_, bf16[4,1024]{1,0:T(4,128)(2,1)S(1)} %get-tuple-element.16.refs_1_, ...), custom_call_target="tpu_custom_call" | custom-call | tf_op jit(solution)/shard_map/pallas_call | solution.py:338
